TPU v7x, 256 devices: a whole 4x4x8 slice. The times are simulated.
256 devices in a mesh: mz: 128 (over y, x_lo, z, core), pix: 2 (over x_hi).
Axes of the slice: x: 4 (x_hi: 2, x_lo: 2; x = x_hi * 2 + x_lo), y: 4, z: 8, core: 2. Of those that a mesh axis runs over, the one named last changes fastest.
Arguments:
- residual: float32 [128, 128, 16384], P('pix', None, 'mz'), may hold values from -6 to 6
- tissue_mask: int32 [128, 128], P('pix'), may hold values 0 or 1
- peak_class: int32 [16384], P('mz'), may hold values from 0 to 3
- peak_taps: float32 [4, 384], replicated, may hold values from -0.3125 to 0.3125
- blur_taps: float32 [9, 9], replicated, may hold values from -0.625 to 0.625
Outputs:
- gradient: float32 [128, 128, 16384], P('pix', None, 'mz')
All inputs are finite; a program needn't handle non-finite values. No bound on the sum of `tissue_mask` on one device may be relied on, other than what follows from the above.
Results may differ from a plain program's by a relative error of at most 0.0003.
Values sent between devices are 32-bit elements; how exact they have to be, the bound alone decides.
A program may use at most 128 MiB of HBM per device.

v0:
```python
import jax
import jax.numpy as jnp
from jax import lax
from jax.sharding import PartitionSpec as P


def from_behind(block, axis, distance):
    devices = range(lax.axis_size(axis))
    route = [(i - distance, i) for i in devices if i - distance in devices]
    return lax.ppermute(block, axis, route)


def padded_2(shard, sides, width):
    for axis, dim in sides:
        count, length = (lax.axis_size(axis), shard.shape[dim])
        up = [(i, (i + 1) % count) for i in range(count - 1)]
        down = [(j, i) for i, j in up]
        last = lax.slice_in_dim(shard, length - width, length, axis=dim)
        leading = lax.slice_in_dim(shard, 0, width, axis=dim)
        before = lax.ppermute(last, axis, up)
        after = lax.ppermute(leading, axis, down)
        shard = jnp.concatenate([before, shard, after], axis=dim)
    return shard


def toeplitz_stack(taps, nrows, ncols, offset_shift):
    length = nrows + ncols
    margin = nrows + ncols
    padded = jnp.pad(taps, ((0, 0), (margin, margin)))
    start = offset_shift - nrows + margin
    window = padded[:, start : start + length]
    rotated = jnp.concatenate([window[:, nrows:], window[:, :nrows]], axis=1)
    tiled = jnp.tile(rotated, (1, nrows))[:, : nrows * (length - 1)]
    return tiled.reshape(taps.shape[0], nrows, length - 1)[:, :, :ncols]


def class_band(classes, peak_taps, ncols, offset_shift):
    stacked = toeplitz_stack(peak_taps, classes.shape[0], ncols, offset_shift)
    band = jnp.zeros((classes.shape[0], ncols), jnp.float32)
    for level in range(peak_taps.shape[0]):
        band = band + jnp.where((classes == level)[:, None], stacked[level], jnp.float32(0.0))
    return band


def near_shift(values, steps):
    return from_behind(values, "mz", steps)


def far_shift(values, steps):
    return from_behind(values, "mz", steps)


def per_device(residual, tissue_mask, peak_class, peak_taps, blur_taps):
    rows, cols, width = residual.shape
    half = peak_taps.shape[1] // 2
    outer = half - width
    masked = (residual * tissue_mask.astype(jnp.float32)[:, :, None]).reshape(rows * cols, width)
    band = class_band(peak_class, peak_taps, 5 * width, half - 2 * width)
    terms = jnp.dot(
        masked, band, precision=lax.Precision.HIGHEST, preferred_element_type=jnp.float32
    )
    left_outer = terms[:, width - outer : width]
    left_part = terms[:, width : 2 * width]
    own_part = terms[:, 2 * width : 3 * width]
    right_part = terms[:, 3 * width : 4 * width]
    right_outer = terms[:, 4 * width : 4 * width + outer]
    spectral = own_part + near_shift(left_part, -1) + near_shift(right_part, 1)
    spectral = spectral + jnp.pad(far_shift(left_outer, -2), ((0, 0), (width - outer, 0)))
    spectral = spectral + jnp.pad(far_shift(right_outer, 2), ((0, 0), (0, width - outer)))
    spectral = spectral.reshape(rows, cols, width)
    framed = padded_2(spectral, (("pix", 0),), 4)
    blur_mats = toeplitz_stack(blur_taps, cols, cols, 4)
    total = jnp.zeros((rows, cols, width), jnp.float32)
    for tap_row in range(9):
        block = framed[8 - tap_row : 8 - tap_row + rows]
        total = total + jnp.einsum(
            "rcb,cd->rdb",
            block,
            blur_mats[tap_row],
            precision=lax.Precision.HIGHEST,
            preferred_element_type=jnp.float32,
        )
    return total


def solution(mesh):
    in_specs = (P("pix", None, "mz"), P("pix", None), P("mz"), P(), P())
    out_specs = P("pix", None, "mz")
    return jax.shard_map(
        per_device, mesh=mesh, in_specs=in_specs, out_specs=out_specs, check_vma=False
    )
```

profile of v0, /device:TPU:25, one launch (start us, length us, event | category | flops | bytes accessed | tf_op | source)
XLA Modules:
  0.0 209.4 jit_solution(13375979025452601662)
XLA Ops:
  4.5 4.0 %broadcast_multiply_fusion = f32[64,128,128]{2,1,0:T(8,128)S(1)} fusion(f32[64,128,128]{2,1,0:T(8,128)} %param.5, f32[64,128]{1,0:T(8,128)S(1)} %convert_element_type.11), kind=kLoop, calls=%fused_computation.41 | loop fusion | flops 1048576 | bytes 8421376 | tf_op jit(solution)/shard_map/mul | solution.py:57
  8.6 18.3 %fusion.39 = f32[8192,640]{1,0:T(8,128)S(1)} fusion(f32[8192,128]{1,0:T(8,128)S(1)} %bitcast.73, f32[4,128,767]{2,1,0:T(8,128)S(1)} %reshape.50, pred[128]{0:T(512)(128)(4,1)S(1)} %get-tuple-element.15, pred[128]{0:T(512)(128)(4,1)S(1)} %get-tuple-element.16, pred[128]{0:T(512)(128)(4,1)S(1)} %get-tuple-element.14, pred[128]{0:T(512)(128)(4,1)S(1)} %get-tuple-element.13), kind=kOutput, calls=%fused_computation.46 | convolution fusion | flops 8053637120 | bytes 26478592 | tf_op jit(solution)/shard_map/dot_general | solution.py:59
  26.9 4.1 %fusion.61 = (f32[8192,128]{1,0:T(8,128)}, f32[8192,128]{1,0:T(8,128)}) fusion(f32[8192,640]{1,0:T(8,128)S(1)} %fusion.39), kind=kLoop, calls=%fused_computation.85 | loop fusion | bytes 16777216 | tf_op jit(solution)/shard_map/slice | solution.py:63
  31.1 4.1 %collective-permute-start.1 = (f32[8192,128]{1,0:T(8,128)}, f32[8192,128]{1,0:T(8,128)}, u32[]{:S(2)}, u32[]{:S(2)}) collective-permute-start(f32[8192,128]{1,0:T(8,128)} %get-tuple-element.8), channel_id=1, source_target_pairs={{0,2},{2,4},{4,6},{6,8},{8,10},{10,12},{12,14},{14,16},{16,18},{18... | collective-permute-start | bytes 12582920 | tf_op jit(solution)/shard_map/ppermute | solution.py:10
  35.2 1.9 collective-permute-start
  37.1 4.5 %fusion.60 = (f32[8192,64]{1,0:T(8,128)}, f32[8192,64]{1,0:T(8,128)}) fusion(f32[8192,640]{1,0:T(8,128)S(1)} %fusion.39), kind=kLoop, calls=%fused_computation.84 | loop fusion | bytes 8388608 | tf_op jit(solution)/shard_map/slice | solution.py:62
  41.6 3.8 %copy.18 = f32[8192,64]{0,1:T(8,128)} copy(f32[8192,64]{1,0:T(8,128)} %get-tuple-element.6) | data formatting | bytes 4194304 | tf_op jit(solution)/shard_map/slice | solution.py:66
  45.5 3.7 %collective-permute-start.3 = (f32[8192,64]{0,1:T(8,128)}, f32[8192,64]{0,1:T(8,128)}, u32[]{:S(2)}, u32[]{:S(2)}) collective-permute-start(f32[8192,64]{0,1:T(8,128)} %copy.18), channel_id=1, source_target_pairs={{0,4},{2,6},{4,8},{6,10},{8,12},{10,14},{12,16},{14,18},{16,20},{1... | collective-permute-start | bytes 6291464 | tf_op jit(solution)/shard_map/ppermute | solution.py:10
  49.2 3.8 %copy.16 = f32[8192,64]{0,1:T(8,128)} copy(f32[8192,64]{1,0:T(8,128)} %get-tuple-element.5) | data formatting | bytes 4194304 | tf_op jit(solution)/shard_map/slice | solution.py:62
  53.0 17.0 %collective-permute-start.2 = (f32[8192,64]{0,1:T(8,128)}, f32[8192,64]{0,1:T(8,128)}, u32[]{:S(2)}, u32[]{:S(2)}) collective-permute-start(f32[8192,64]{0,1:T(8,128)} %copy.16), channel_id=1, source_target_pairs={{4,0},{6,2},{8,4},{10,6},{12,8},{14,10},{16,12},{18,14},{20,16},{2... | collective-permute-start | bytes 6291464 | tf_op jit(solution)/shard_map/ppermute | solution.py:10
  73.2 57.6 %collective-permute-done.3 = f32[8192,64]{0,1:T(8,128)} collective-permute-done((f32[8192,64]{0,1:T(8,128)}, f32[8192,64]{0,1:T(8,128)}, u32[]{:S(2)}, u32[]{:S(2)}) %collective-permute-start.3) | collective-permute-done | bytes 2097184 | tf_op jit(solution)/shard_map/ppermute | solution.py:10
  130.8 3.9 %copy.19 = f32[8192,64]{1,0:T(8,128)} copy(f32[8192,64]{0,1:T(8,128)} %collective-permute-done.3) | data formatting | bytes 4194304 | tf_op jit(solution)/shard_map/ppermute | solution.py:10
  134.7 3.8 %copy.17 = f32[8192,64]{1,0:T(8,128)} copy(f32[8192,64]{0,1:T(8,128)} %collective-permute-done.2) | data formatting | bytes 4194304 | tf_op jit(solution)/shard_map/ppermute | solution.py:10
  138.5 8.2 %fusion.30 = f32[8192,128]{1,0:T(8,128)S(1)} fusion(f32[8192,128]{1,0:T(8,128)} %collective-permute-done.1, f32[8192,128]{1,0:T(8,128)} %collective-permute-done, f32[8192,640]{1,0:T(8,128)} %copy-done, f32[8192,64]{1,0:T(8,128)} %copy.19, f32[8192,64]{1,0:T(8,128)} %copy.17), kind=kLoop, calls=%fused_computation.33 | loop fusion | flops 4194304 | bytes 20971520 | tf_op jit(solution)/shard_map/add | solution.py:69
  146.8 4.4 %collective-permute-start.5 = (f32[4,128,128]{2,1,0:T(8,128)S(1)}, f32[4,128,128]{2,1,0:T(8,128)S(1)}, u32[]{:S(2)}, u32[]{:S(2)}) collective-permute-start(f32[4,128,128]{2,1,0:T(8,128)S(1)} %bitcast.78), channel_id=1, source_target_pairs={{0,1},{2,3},{4,5},{6,7},{8,9},{10,11},{12,13},{14,15},{16,17},{18,... | collective-permute-start | bytes 786440 | tf_op jit(solution)/shard_map/ppermute | solution.py:20
  152.5 5.2 %fusion.50 = f32[128,64,128]{2,0,1:T(8,128)} fusion(f32[64,128,128]{2,1,0:T(8,128)S(1)} %bitcast.64, f32[9,128,255]{2,1,0:T(8,128)S(1)} %reshape.48), kind=kOutput, calls=%fused_computation.62 | convolution fusion | flops 1610612736 | bytes 8454144 | tf_op jit(solution)/shard_map/rcb,cd->rdb/dot_general | solution.py:76
  157.7 5.2 %fusion.1 = f32[128,64,128]{2,0,1:T(8,128)} fusion(f32[4,128,128]{2,1,0:T(8,128)S(1)} %collective-permute-done.5, f32[64,128,128]{2,1,0:T(8,128)S(1)} %bitcast.65, f32[9,128,255]{2,1,0:T(8,128)S(1)} %reshape.48), kind=kOutput, calls=%fused_computation.7 | convolution fusion | flops 1611661312 | bytes 8716288 | tf_op jit(solution)/shard_map/rcb,cd->rdb/dot_general | solution.py:76
  162.9 5.2 %fusion.7 = f32[128,64,128]{2,0,1:T(8,128)} fusion(f32[4,128,128]{2,1,0:T(8,128)S(1)} %collective-permute-done.5, f32[64,128,128]{2,1,0:T(8,128)S(1)} %bitcast.66, f32[9,128,255]{2,1,0:T(8,128)S(1)} %reshape.48), kind=kOutput, calls=%fused_computation.11 | convolution fusion | flops 1611661312 | bytes 8716288 | tf_op jit(solution)/shard_map/rcb,cd->rdb/dot_general | solution.py:76
  168.1 5.2 %fusion.4 = f32[128,64,128]{2,0,1:T(8,128)} fusion(f32[4,128,128]{2,1,0:T(8,128)S(1)} %collective-permute-done.5, f32[64,128,128]{2,1,0:T(8,128)S(1)} %bitcast.67, f32[9,128,255]{2,1,0:T(8,128)S(1)} %reshape.48), kind=kOutput, calls=%fused_computation.9 | convolution fusion | flops 1611661312 | bytes 8716288 | tf_op jit(solution)/shard_map/rcb,cd->rdb/dot_general | solution.py:76
  173.3 5.1 %fusion.23 = f32[128,64,128]{2,0,1:T(8,128)} fusion(f32[4,128,128]{2,1,0:T(8,128)S(1)} %collective-permute-done.4, f32[64,128,128]{2,1,0:T(8,128)S(1)} %bitcast.68, f32[9,128,255]{2,1,0:T(8,128)S(1)} %reshape.48), kind=kOutput, calls=%fused_computation.25 | convolution fusion | flops 1611661312 | bytes 8716288 | tf_op jit(solution)/shard_map/rcb,cd->rdb/dot_general | solution.py:76
  178.3 5.1 %fusion.10 = f32[128,64,128]{2,0,1:T(8,128)} fusion(f32[4,128,128]{2,1,0:T(8,128)S(1)} %collective-permute-done.4, f32[64,128,128]{2,1,0:T(8,128)S(1)} %bitcast.69, f32[9,128,255]{2,1,0:T(8,128)S(1)} %reshape.48), kind=kOutput, calls=%fused_computation.13 | convolution fusion | flops 1611661312 | bytes 8716288 | tf_op jit(solution)/shard_map/rcb,cd->rdb/dot_general | solution.py:76
  183.5 5.1 %fusion.13 = f32[128,64,128]{2,0,1:T(8,128)} fusion(f32[4,128,128]{2,1,0:T(8,128)S(1)} %collective-permute-done.4, f32[64,128,128]{2,1,0:T(8,128)S(1)} %bitcast.70, f32[9,128,255]{2,1,0:T(8,128)S(1)} %reshape.48), kind=kOutput, calls=%fused_computation.15 | convolution fusion | flops 1611661312 | bytes 8716288 | tf_op jit(solution)/shard_map/rcb,cd->rdb/dot_general | solution.py:76
  188.6 5.1 %fusion.16 = f32[128,64,128]{2,0,1:T(8,128)} fusion(f32[4,128,128]{2,1,0:T(8,128)S(1)} %collective-permute-done.4, f32[64,128,128]{2,1,0:T(8,128)S(1)} %bitcast.71, f32[9,128,255]{2,1,0:T(8,128)S(1)} %reshape.48), kind=kOutput, calls=%fused_computation.17 | convolution fusion | flops 1611661312 | bytes 8716288 | tf_op jit(solution)/shard_map/rcb,cd->rdb/dot_general | solution.py:76
  193.7 15.5 %add_bitcast_fusion = f32[64,128,128]{2,1,0:T(8,128)} fusion(f32[128,64,128]{2,0,1:T(8,128)} %fusion.1, f32[128,64,128]{2,0,1:T(8,128)} %fusion.7, f32[128,64,128]{2,0,1:T(8,128)} %fusion.4, f32[128,64,128]{2,0,1:T(8,128)} %fusion.50, f32[128,64,128]{2,0,1:T(8,128)} %fusion.23, f32[128,64,128]{2,0,1:T(8,128)} %fusion.10, f32[128,64,128]{2,0,1:T(8,128)} %fusion.13, ...), kind=kOutput, calls=%fused_computation.34 | convolution fusion | flops 1620049920 | bytes 42270720 | tf_op jit(solution)/shard_map/rcb,cd->rdb/dot_general | solution.py:76
  (28 shorter events, 9.0 us)
Async XLA Ops:
  1.7 2.9 %copy-start.2 = (s32[128]{0:T(128)S(1)}, s32[128]{0:T(128)}, u32[]{:S(2)}) copy-start(s32[128]{0:T(128)} %param.7) | copy-start | bytes 1540
  26.9 14.7 %copy-start = (f32[8192,640]{1,0:T(8,128)}, f32[8192,640]{1,0:T(8,128)S(1)}, u32[]{:S(2)}) copy-start(f32[8192,640]{1,0:T(8,128)S(1)} %fusion.39) | copy-start | bytes 62914564
  31.1 107.4 %collective-permute-start.1 = (f32[8192,128]{1,0:T(8,128)}, f32[8192,128]{1,0:T(8,128)}, u32[]{:S(2)}, u32[]{:S(2)}) collective-permute-start(f32[8192,128]{1,0:T(8,128)} %get-tuple-element.8), channel_id=1, source_target_pairs={{0,2},{2,4},{4,6},{6,8},{8,10},{10,12},{12,14},{14,16},{16,18},{18... | collective-permute-start | bytes 12582920 | tf_op jit(solution)/shard_map/ppermute | solution.py:10
  35.2 103.3 %collective-permute-start = (f32[8192,128]{1,0:T(8,128)}, f32[8192,128]{1,0:T(8,128)}, u32[]{:S(2)}, u32[]{:S(2)}) collective-permute-start(f32[8192,128]{1,0:T(8,128)} %get-tuple-element.7), channel_id=1, source_target_pairs={{2,0},{4,2},{6,4},{8,6},{10,8},{12,10},{14,12},{16,14},{18,16},{20... | collective-permute-start | bytes 12582920 | tf_op jit(solution)/shard_map/ppermute | solution.py:10
  45.5 24.5 %copy-start.1 = (f32[9,9]{1,0:T(8,128)S(1)}, f32[9,9]{1,0:T(8,128)}, u32[]{:S(2)}) copy-start(f32[9,9]{1,0:T(8,128)} %param.9) | copy-start | bytes 976
  45.5 85.3 %collective-permute-start.3 = (f32[8192,64]{0,1:T(8,128)}, f32[8192,64]{0,1:T(8,128)}, u32[]{:S(2)}, u32[]{:S(2)}) collective-permute-start(f32[8192,64]{0,1:T(8,128)} %copy.18), channel_id=1, source_target_pairs={{0,4},{2,6},{4,8},{6,10},{8,12},{10,14},{12,16},{14,18},{16,20},{1... | collective-permute-start | bytes 6291464 | tf_op jit(solution)/shard_map/ppermute | solution.py:10
  53.0 81.7 %collective-permute-start.2 = (f32[8192,64]{0,1:T(8,128)}, f32[8192,64]{0,1:T(8,128)}, u32[]{:S(2)}, u32[]{:S(2)}) collective-permute-start(f32[8192,64]{0,1:T(8,128)} %copy.16), channel_id=1, source_target_pairs={{4,0},{6,2},{8,4},{10,6},{12,8},{14,10},{16,12},{18,14},{20,16},{2... | collective-permute-start | bytes 6291464 | tf_op jit(solution)/shard_map/ppermute | solution.py:10
  146.8 10.9 %collective-permute-start.5 = (f32[4,128,128]{2,1,0:T(8,128)S(1)}, f32[4,128,128]{2,1,0:T(8,128)S(1)}, u32[]{:S(2)}, u32[]{:S(2)}) collective-permute-start(f32[4,128,128]{2,1,0:T(8,128)S(1)} %bitcast.78), channel_id=1, source_target_pairs={{0,1},{2,3},{4,5},{6,7},{8,9},{10,11},{12,13},{14,15},{16,17},{18,... | collective-permute-start | bytes 786440 | tf_op jit(solution)/shard_map/ppermute | solution.py:20
  151.2 22.1 %collective-permute-start.4 = (f32[4,128,128]{2,1,0:T(8,128)S(1)}, f32[4,128,128]{2,1,0:T(8,128)S(1)}, u32[]{:S(2)}, u32[]{:S(2)}) collective-permute-start(f32[4,128,128]{2,1,0:T(8,128)S(1)} %bitcast.77), channel_id=1, source_target_pairs={{1,0},{3,2},{5,4},{7,6},{9,8},{11,10},{13,12},{15,14},{17,16},{19,... | collective-permute-start | bytes 786440 | tf_op jit(solution)/shard_map/ppermute | solution.py:21
where the time goes:
time: 214 us; the launch traced here: 209 us
  matrix products  75.1 us (35%)
  waiting for transfers between devices  57.6 us (27%)
  starting transfers between devices  32.3 us (15%)
  local copies, waits for them, and re-layouts  31 us (14%)
  other arithmetic  13 us (6%)
    ppermute x4, waiting for transfers between devices, from_behind(): return lax.ppermute(block, axis, route)  57.6 us
    dot_general x9, matrix products, per_device(): jnp.einsum('rcb,cd->rdb', block, blur_mats[tap_row], precision=lax.Precis...  56.7 us
    ppermute x4, starting transfers between devices, from_behind(): return lax.ppermute(block, axis, route)  26.7 us
    dot_general x1, matrix products, per_device(): jnp.dot(masked, band, precision=lax.Precision.HIGHEST, preferred_element_...  18.3 us
    slice x2, local copies, waits for them, and re-layouts, per_device(): left_outer = terms[:, width - outer:width]  8.33 us
    add x1, other arithmetic, per_device(): spectral + jnp.pad(far_shift(right_outer, 2), ((0, 0), (0, width - outer)))  8.21 us
    ppermute x2, local copies, waits for them, and re-layouts, from_behind(): return lax.ppermute(block, axis, route)  7.69 us
    ppermute x1, starting transfers between devices, padded_2(): before = lax.ppermute(last, axis, up)  4.37 us
  transfers between devices with their start and end apart: 6, of which 1 were waited for; matrix products, arithmetic and copies ran while one was open for 21% of the time, Pallas kernels for 0%

commit v1 on v0

v1 whole, which is shorter than its diff:
```python
import functools

import jax
import jax.numpy as jnp
from jax import lax
from jax.experimental import pallas as pl
from jax.experimental.pallas import tpu as pltpu
from jax.sharding import PartitionSpec as P

MESH = pl.DeviceIdType.MESH
F32 = jnp.float32
BF16 = jnp.bfloat16
WIDTH = 128
COLS = 128
STEP = 4
AHEAD = 3
FAR_AHEAD = 8
EDGE_AT = 14
LINE = 16


def split(values):
    high = values.astype(BF16)
    return high, (values - high.astype(F32)).astype(BF16)


def dot(a, b):
    return jnp.dot(a, b, preferred_element_type=F32)


def column(row):
    return jnp.broadcast_to(row, (WIDTH, row.shape[1])).T


def kernel(
    slabs, rows,
    x_ref, mask_hbm, class_hbm, taps_hbm, blur_hbm, out_ref,
    mask_ref, class_ref, taps_ref, blur_ref, own, far, near, beyond, half, packed, spectral, blur_high, blur_low,
    stack, band, half_high, half_low, edge_out, edge_in, classes,
    small_sem, own_sem, far_send, far_recv, near_send, near_recv, on_send, on_recv,
    half_send, half_recv, edge_sems, class_send, class_recv,
):
    m = lax.axis_index("mz")
    pix = lax.axis_index("pix")
    core = lax.rem(m, 2)
    side = 1 - 2 * core
    partner, next_chip, two_on, two_back = (m + side, m - side, m + 2 * side, m - 2 * side)
    inside = (m > 0) & (m < slabs - 1)
    late = (lax.rem(m, LINE) < 2) | (lax.rem(m, LINE) >= LINE - 2)
    sends_half = (two_on >= 0) & (two_on < slabs)
    chunks = rows // STEP
    size = STEP * COLS

    def base(c):
        return jnp.where(pix == 0, rows - STEP * (c + 1), STEP * c)

    def at(c):
        return pl.ds(base(c), STEP)

    def remote(src, dst, send, recv, to):
        return pltpu.make_async_remote_copy(
            src_ref=src, dst_ref=dst, send_sem=send, recv_sem=recv,
            device_id=to, device_id_type=MESH,
        )

    def load_own(c):
        return pltpu.make_async_copy(x_ref.at[at(c)], own.at[at(c)], own_sem.at[c])

    def to_far(c):
        return remote(x_ref.at[at(c)], far.at[at(c)], far_send.at[c], far_recv.at[c], (next_chip, pix))

    def to_near(c):
        return remote(x_ref.at[at(c)], near.at[at(c)], near_send.at[c], near_recv.at[c], (partner, pix))

    def pass_on(c):
        return remote(far.at[at(c)], beyond.at[at(c)], on_send.at[c], on_recv.at[c], (partner, pix))

    def to_half(c):
        return remote(packed.at[c], half.at[c], half_send.at[c], half_recv.at[c], (two_on, pix))

    def to_edge():
        return remote(edge_out, edge_in, edge_sems.at[0], edge_sems.at[1], (m, 1 - pix))

    def class_copy(src, slot, to):
        return remote(classes.at[src], classes.at[slot], class_send.at[slot], class_recv.at[slot], (to, pix))

    class_near = class_copy(0, 1, partner)
    class_far = class_copy(0, 2, next_chip)
    class_half = class_copy(0, 3, two_on)
    class_on = class_copy(2, 4, partner)

    barrier = pltpu.get_barrier_semaphore()
    pl.semaphore_signal(barrier, inc=1, device_id=(partner, pix), device_id_type=MESH)
    pl.semaphore_signal(barrier, inc=1, device_id=(m, 1 - pix), device_id_type=MESH)

    @pl.when(inside)
    def _():
        pl.semaphore_signal(barrier, inc=1, device_id=(next_chip, pix), device_id_type=MESH)
        pl.semaphore_signal(barrier, inc=1, device_id=(two_back, pix), device_id_type=MESH)

    def loop(count, body):
        lax.fori_loop(0, count, lambda i, carry: (body(i), carry)[1], 0)

    small = [
        pltpu.make_async_copy(src, dst, small_sem.at[i])
        for i, (src, dst) in enumerate(
            ((class_hbm, class_ref), (blur_hbm, blur_ref), (taps_hbm, taps_ref), (mask_hbm, mask_ref))
        )
    ]
    for copy in small:
        copy.start()
    loop(chunks, lambda c: load_own(c).start())
    small[0].wait()
    classes[0] = jnp.broadcast_to(class_ref[...], (8, WIDTH))
    pl.semaphore_wait(barrier, 2 + inside.astype(jnp.int32) + sends_half.astype(jnp.int32))

    @pl.when(inside)
    def _():
        class_far.start()
        loop(FAR_AHEAD, lambda c: to_far(c).start())

    class_near.start()

    @pl.when(sends_half)
    def _():
        class_half.start()

    low_lanes = lax.broadcasted_iota(jnp.int32, (size // 2, WIDTH), 1) < WIDTH // 2
    rolled_lanes = low_lanes == (core == 0)

    def pack(c):
        load_own(c).wait()
        to_near(c).start()
        pair = STEP // 2
        moved = own[pl.ds(base(c) + pair * core, pair)].reshape(size // 2, WIDTH)
        stays = own[pl.ds(base(c) + pair * (1 - core), pair)].reshape(size // 2, WIDTH)
        packed[c] = jnp.where(rolled_lanes, pltpu.roll(moved, WIDTH // 2, 1), stays)

        @pl.when(sends_half)
        def _():
            to_half(c).start()

    loop(AHEAD, pack)
    for copy in small[1:]:
        copy.wait()

    blur_high[...] = jnp.zeros_like(blur_high)
    blur_low[...] = jnp.zeros_like(blur_low)
    offset = (
        lax.broadcasted_iota(jnp.int32, (COLS, COLS), 0)
        - lax.broadcasted_iota(jnp.int32, (COLS, COLS), 1)
        + 4
    )
    for a in range(9):
        toeplitz = jnp.zeros((COLS, COLS), F32)
        for b in range(9):
            toeplitz = jnp.where(offset == b, blur_ref[a, b], toeplitz)
        high, low = split(toeplitz)
        for r in range(STEP):
            place = (slice(r * COLS, (r + 1) * COLS), slice((r + 8 - a) * COLS, (r + 9 - a) * COLS))
            blur_high[place] = high
            blur_low[place] = low

    taps = taps_ref.shape[1]
    for k in range(taps_ref.shape[0]):
        wide = jnp.concatenate(
            [jnp.broadcast_to(taps_ref[k : k + 1, :], (WIDTH, taps)), jnp.zeros((WIDTH, 5 * WIDTH - taps), F32)], axis=1
        )
        wide = pltpu.roll(wide, WIDTH // 2, 1, stride=1, stride_axis=0)
        for block in range(5):
            stack[k, block] = wide[:, block * WIDTH : (block + 1) * WIDTH]

    def weights(slot, block):
        level = column(classes[slot, 0:1, :])
        total = jnp.zeros((WIDTH, WIDTH), F32)
        for k in range(taps_ref.shape[0]):
            total = total + jnp.where(level == k, stack[k, block], F32(0.0))
        return total

    def keep(place, slot, block):
        high, low = split(weights(slot, block))
        band[place * WIDTH : (place + 1) * WIDTH, :WIDTH] = high
        band[place * WIDTH : (place + 1) * WIDTH, WIDTH:] = low

    @pl.when(inside)
    def _():
        class_far.wait_recv()
        class_half.wait_recv()

    @pl.when(jnp.logical_not(inside))
    def _():
        classes[2] = jnp.zeros_like(classes[2])
        classes[3] = jnp.zeros_like(classes[3])

    class_on.start()
    keep(0, 0, 2)
    class_near.wait_recv()
    keep(1, 1, 1 + 2 * core)
    keep(2, 2, 3 - 2 * core)
    outer = weights(3, 4 - 4 * core)
    other = pltpu.roll(outer, WIDTH // 2, 0)
    for place, value in ((0, jnp.where(core == 0, other, outer)), (1, jnp.where(core == 0, outer, other))):
        high, low = split(value)
        half_high[:, place * WIDTH : (place + 1) * WIDTH] = high
        half_low[:, place * WIDTH : (place + 1) * WIDTH] = low
    class_on.wait_recv()
    keep(3, 4, 4 * core)

    def keep_spectral(row, values):
        high, low = split(values)
        place = pl.ds(pl.multiple_of(row * COLS, size), size)
        spectral[place, :WIDTH] = high
        spectral[place, WIDTH:] = low

    keep_spectral(jnp.where(pix == 0, 0, rows + 4), jnp.zeros((size, WIDTH), F32))

    def banded(c, refs, first):
        rows_of = slice(first * WIDTH, (first + 2) * WIDTH)
        high, low = split(jnp.concatenate([ref[at(c)].reshape(size, WIDTH) for ref in refs], axis=1))
        both = dot(high, band[rows_of, :])
        return both[:, :WIDTH] + both[:, WIDTH:] + dot(low, band[rows_of, :WIDTH])

    def early_part(c):
        high, low = split(half[c])
        extra = dot(high, half_high[...]) + dot(high, half_low[...]) + dot(low, half_high[...])
        return banded(c, (own, near), 0) + jnp.concatenate([extra[:, :WIDTH], extra[:, WIDTH:]], axis=0)

    def late_part(c):
        return banded(c, (far, beyond), 2)

    def tissue(c):
        rows_of = [column(mask_ref[pl.ds(base(c) + r, 1), :].astype(F32)) for r in range(STEP)]
        return jnp.concatenate(rows_of, axis=0)

    def window(c, start, groups):
        lanes = pl.ds(pl.multiple_of(start * size, size), groups * size)
        place = pl.ds(pl.multiple_of(base(c) * COLS + start * size, size), groups * size)
        both = dot(blur_high[:, lanes], spectral[place, :])
        return both[:, :WIDTH] + both[:, WIDTH:] + dot(blur_low[:, lanes], spectral[place, :WIDTH])

    def keep_out(c, values):
        out_ref[at(c)] = values.reshape(STEP, COLS, WIDTH)

    def blur(c):
        keep_out(c, window(c, 0, 3))

    def arrive_near(c):
        to_near(c).wait_recv()

        @pl.when(inside)
        def _():
            to_half(c).wait_recv()

        @pl.when(jnp.logical_not(inside))
        def _():
            half[c] = jnp.zeros((size // 2, WIDTH), F32)

    def arrive_far(c):
        @pl.when(inside)
        def _():
            to_far(c).wait_recv()

        @pl.when(jnp.logical_not(inside))
        def _():
            far[at(c)] = jnp.zeros((STEP, COLS, WIDTH), F32)

        pass_on(c).start()

    def take_edge():
        to_edge().wait_recv()
        keep_spectral(jnp.where(pix == 0, rows + 4, 0), edge_in[...])
        blur(0)

    def step(c):
        @pl.when(inside & (c + FAR_AHEAD < chunks))
        def _():
            to_far(c + FAR_AHEAD).start()

        @pl.when(c + AHEAD < chunks)
        def _():
            pack(c + AHEAD)

        @pl.when(c >= 3)
        def _():
            blur(c - 2)

        @pl.when(jnp.logical_not(late) & (c == EDGE_AT))
        def _():
            take_edge()

        arrive_far(c)
        arrive_near(c)
        values = early_part(c)
        pass_on(c).wait_recv()
        values = (values + late_part(c)) * tissue(c)
        keep_spectral(base(c) + 4, values)

        @pl.when(c == 0)
        def _():
            edge_out[...] = values

        @pl.when(jnp.logical_not(late) & (c == 0))
        def _():
            to_edge().start()

    last = chunks - 1
    loop(last, step)

    blur(last - 2)
    keep_out(last - 1, window(last - 1, 1 - pix, 2))
    keep_out(last, window(last, 2 - 2 * pix, 1))
    arrive_far(last)

    @pl.when(late)
    def _():
        to_edge().start()

    arrive_near(last)
    values = early_part(last)
    cover = tissue(last)
    pass_on(last).wait_recv()
    keep_spectral(base(last) + 4, (values + late_part(last)) * cover)
    for c, start in ((last - 1, 2 * pix), (last, 1)):
        out_ref[at(c)] = out_ref[at(c)] + window(c, start, 1).reshape(STEP, COLS, WIDTH)

    @pl.when(late)
    def _():
        take_edge()

    to_edge().wait_send()
    class_near.wait_send()
    class_on.wait_send()

    @pl.when(inside)
    def _():
        class_far.wait_send()
        loop(chunks, lambda c: to_far(c).wait_send())

    @pl.when(sends_half)
    def _():
        class_half.wait_send()
        loop(chunks, lambda c: to_half(c).wait_send())

    def finish(c):
        to_near(c).wait_send()
        pass_on(c).wait_send()

    loop(chunks, finish)


def per_device(residual, tissue_mask, peak_class, peak_taps, blur_taps):
    rows, cols, width = residual.shape
    chunks = rows // STEP
    size = STEP * cols
    slabs = lax.axis_size("mz")
    block = (rows, cols, width)
    dma = pltpu.SemaphoreType.DMA
    return pl.pallas_call(
        functools.partial(kernel, slabs, rows),
        out_shape=jax.ShapeDtypeStruct(block, F32),
        in_specs=[pl.BlockSpec(memory_space=pltpu.HBM)] * 5,
        out_specs=pl.BlockSpec(memory_space=pltpu.VMEM),
        scratch_shapes=[
            pltpu.VMEM(tissue_mask.shape, jnp.int32),
            pltpu.VMEM((1, width), jnp.int32),
            pltpu.VMEM(peak_taps.shape, F32),
            pltpu.SMEM(blur_taps.shape, F32),
            pltpu.VMEM(block, F32),
            pltpu.VMEM(block, F32),
            pltpu.VMEM(block, F32),
            pltpu.VMEM(block, F32),
            pltpu.VMEM((chunks, size // 2, width), F32),
            pltpu.VMEM((chunks, size // 2, width), F32),
            pltpu.VMEM(((rows + 8) * cols, 2 * width), BF16),
            pltpu.VMEM((size, (STEP + 8) * cols), BF16),
            pltpu.VMEM((size, (STEP + 8) * cols), BF16),
            pltpu.VMEM((peak_taps.shape[0], 5, width, width), F32),
            pltpu.VMEM((4 * width, 2 * width), BF16),
            pltpu.VMEM((width, 2 * width), BF16),
            pltpu.VMEM((width, 2 * width), BF16),
            pltpu.VMEM((size, width), F32),
            pltpu.VMEM((size, width), F32),
            pltpu.VMEM((5, 8, width), jnp.int32),
            dma((4,)),
            dma((chunks,)),
            dma((chunks,)),
            dma((chunks,)),
            dma((chunks,)),
            dma((chunks,)),
            dma((chunks,)),
            dma((chunks,)),
            dma((chunks,)),
            dma((chunks,)),
            dma((2,)),
            dma((5,)),
            dma((5,)),
        ],
        compiler_params=pltpu.CompilerParams(
            collective_id=0, has_side_effects=True, vmem_limit_bytes=48 * 2**20
        ),
    )(residual, tissue_mask, peak_class.reshape(1, width), peak_taps, blur_taps)


def solution(mesh):
    in_specs = (P("pix", None, "mz"), P("pix", None), P("mz"), P(), P())
    out_specs = P("pix", None, "mz")
    return jax.shard_map(
        per_device, mesh=mesh, in_specs=in_specs, out_specs=out_specs, check_vma=False
    )
```

time: 214 us -> 94.2 us (0.44); the launches traced: 209 us -> 94 us
  Pallas kernels: 0 us -> 89.2 us
  matrix products: 75.1 us -> 0 us
  waiting for transfers between devices: 57.6 us -> 0 us
  starting transfers between devices: 32.3 us -> 0 us
  local copies, waits for them, and re-layouts: 31 us -> 4.82 us
  other arithmetic: 13 us -> 0 us
    pallas_call x0 -> x1, Pallas kernels: none -> 89.2 us  [per_device(): pl.pallas_call(functools.partial(kernel, slabs, rows), out_shape=jax.Shap...]
    dot_general x10 -> x0, matrix products: 75.1 us -> none  [the longest x9 56.7 us: per_device(): jnp.einsum('rcb,cd->rdb', block, blur_mats[tap_row], precision=lax.Precis...]
    ppermute x6 -> x0, waiting for transfers between devices: 57.6 us -> none  [the longest x4 57.6 us: from_behind(): return lax.ppermute(block, axis, route)]
    ppermute x6 -> x0, starting transfers between devices: 32.3 us -> none  [the longest x4 26.7 us: from_behind(): return lax.ppermute(block, axis, route)]
    slice x9 -> x0, local copies, waits for them, and re-layouts: 17.4 us -> none  [the longest x2 8.33 us: per_device(): left_outer = terms[:, width - outer:width]]
    add x1 -> x0, other arithmetic: 8.21 us -> none  [per_device(): spectral + jnp.pad(far_shift(right_outer, 2), ((0, 0), (0, width - outer)))]
    ppermute x2 -> x0, local copies, waits for them, and re-layouts: 7.69 us -> none  [from_behind(): return lax.ppermute(block, axis, route)]
    mul x1 -> x0, other arithmetic: 4.05 us -> none  [per_device(): residual * tissue_mask.astype(jnp.float32)[:, :, None]]
  transfers between devices with their start and end apart: 6 -> 0, of which waited for: 1 -> 0; matrix products, arithmetic and copies ran while one was open for 21% -> 0% of each run, Pallas kernels for 0% -> 0%
where the time goes in v1:
time: 94.2 us; the launch traced here: 94 us
  Pallas kernels  89.2 us (95%)
  local copies, waits for them, and re-layouts  4.82 us (5%)
    pallas_call x1, Pallas kernels, per_device(): pl.pallas_call(functools.partial(kernel, slabs, rows), out_shape=jax.Shap...  89.2 us
    unnamed x9, local copies, waits for them, and re-layouts  4.82 us

profile of v1, /device:TPU:25, one launch (start us, length us, event | category | flops | bytes accessed | tf_op | source)
XLA Modules:
  0.0 94.0 jit_solution(5048271412533007030)
XLA Ops:
  0.0 0.0 copy-start
  0.0 0.8 copy-done
  0.8 0.0 copy-start.1
  0.8 0.7 copy-done.1
  1.5 0.0 copy-start.2
  1.5 0.7 copy-done.2
  2.1 0.0 copy-start.3
  2.2 0.7 copy-done.3
  2.8 89.2 %shard_map.55 = f32[64,128,128]{2,1,0:T(8,128)S(1)} custom-call(f32[64,128,128]{2,1,0:T(8,128)} %x_ref.1, s32[64,128]{1,0:T(8,128)S(1)} %copy-done, s32[1,128]{1,0:T(1,128)S(1)} %bitcast.1, f32[4,384]{1,0:T(4,128)S(1)} %copy-done.2, f32[9,9]{1,0:T(8,128)S(1)} %copy-done.1), custom_call_target="tpu_custom_call" | custom-call | tf_op jit(solution)/shard_map/pallas_call | solution.py:358
  92.0 2.0 %copy.7 = f32[64,128,128]{2,1,0:T(8,128)} copy(f32[64,128,128]{2,1,0:T(8,128)S(1)} %shard_map.55) | data formatting | bytes 8388608
Async XLA Ops:
  0.0 0.8 copy-start
  0.8 0.7 copy-start.1
  1.5 0.7 copy-start.2
  2.1 0.7 copy-start.3

commit v2 on v1

--- a/solution.py
+++ b/solution.py
@@ -12,9 +12,11 @@
 BF16 = jnp.bfloat16
 WIDTH = 128
 COLS = 128
+CLASSES = 4
 STEP = 4
 AHEAD = 3
-FAR_AHEAD = 8
+FAR_AHEAD = 4
+RELAY_AT = 7
 EDGE_AT = 14
 LINE = 16
 
@@ -32,13 +34,27 @@
     return jnp.broadcast_to(row, (WIDTH, row.shape[1])).T
 
 
+def gather_small(mask_hbm, class_hbm, blur_hbm, taps_hbm, out_ref, mask_ref, class_ref, blur_ref, taps_ref, sems):
+    pairs = ((mask_hbm, mask_ref), (class_hbm, class_ref), (blur_hbm, blur_ref), (taps_hbm, taps_ref))
+    copies = [pltpu.make_async_copy(src, dst, sems.at[i]) for i, (src, dst) in enumerate(pairs)]
+    for copy in copies:
+        copy.start()
+    for copy in copies:
+        copy.wait()
+    rows = mask_ref.shape[0]
+    out_ref[:rows] = mask_ref[...].astype(F32)
+    out_ref[rows : rows + 8] = jnp.broadcast_to(class_ref[...].astype(F32), (8, WIDTH))
+    out_ref[rows + 8 : rows + 17, :9] = blur_ref[...]
+    for i in range(3):
+        out_ref[rows + 24 + 4 * i : rows + 28 + 4 * i] = taps_ref[:, i * WIDTH : (i + 1) * WIDTH]
+
+
 def kernel(
     slabs, rows,
-    x_ref, mask_hbm, class_hbm, taps_hbm, blur_hbm, out_ref,
-    mask_ref, class_ref, taps_ref, blur_ref, own, far, near, beyond, half, packed, spectral, blur_high, blur_low,
-    stack, band, half_high, half_low, edge_out, edge_in, classes,
+    x_ref, small_ref, out_ref, blur_ref, own, far, near, beyond, half, packed, spectral, blur_high, blur_low,
+    stack, band, half_high, half_low, edge_out, edge_in, relay, classes,
     small_sem, own_sem, far_send, far_recv, near_send, near_recv, on_send, on_recv,
-    half_send, half_recv, edge_sems, class_send, class_recv,
+    half_send, half_recv, edge_sems, class_send, class_recv, ready,
 ):
     m = lax.axis_index("mz")
     pix = lax.axis_index("pix")
@@ -46,8 +62,20 @@
     side = 1 - 2 * core
     partner, next_chip, two_on, two_back = (m + side, m - side, m + 2 * side, m - 2 * side)
     inside = (m > 0) & (m < slabs - 1)
-    late = (lax.rem(m, LINE) < 2) | (lax.rem(m, LINE) >= LINE - 2)
     sends_half = (two_on >= 0) & (two_on < slabs)
+    place_on_line = lax.rem(m, LINE)
+    follows = (place_on_line < 2) & (m >= LINE)
+    ends = place_on_line >= LINE - 2
+    line_end = (place_on_line < 2) | ends
+    relayed = follows | ends
+    inward = jnp.where(place_on_line < 2, m + 2, m - 2)
+    relays = ((place_on_line >= 2) & (place_on_line < 4) & (m >= LINE)) | (
+        (place_on_line >= LINE - 4) & (place_on_line < LINE - 2)
+    )
+    relays_for = jnp.where(place_on_line < 4, m - 2, m + 2)
+    calls_up = (place_on_line == LINE - 1) & (m < slabs - 1)
+    far_later = follows & (core == 0)
+    half_later = follows & (core == 1)
     chunks = rows // STEP
     size = STEP * COLS
 
@@ -81,6 +109,17 @@
     def to_edge():
         return remote(edge_out, edge_in, edge_sems.at[0], edge_sems.at[1], (m, 1 - pix))
 
+    first, second = pl.ds(0, size // 2), pl.ds(size // 2, size // 2)
+
+    def to_edge_half():
+        return remote(edge_out.at[second], edge_in.at[second], edge_sems.at[0], edge_sems.at[1], (m, 1 - pix))
+
+    def to_relay():
+        return remote(edge_out.at[first], relay, edge_sems.at[2], edge_sems.at[3], (inward, 1 - pix))
+
+    def from_relay():
+        return remote(relay, edge_in.at[first], edge_sems.at[4], edge_sems.at[5], (relays_for, pix))
+
     def class_copy(src, slot, to):
         return remote(classes.at[src], classes.at[slot], class_send.at[slot], class_recv.at[slot], (to, pix))
 
@@ -93,42 +132,50 @@
     pl.semaphore_signal(barrier, inc=1, device_id=(partner, pix), device_id_type=MESH)
     pl.semaphore_signal(barrier, inc=1, device_id=(m, 1 - pix), device_id_type=MESH)
 
-    @pl.when(inside)
-    def _():
-        pl.semaphore_signal(barrier, inc=1, device_id=(next_chip, pix), device_id_type=MESH)
-        pl.semaphore_signal(barrier, inc=1, device_id=(two_back, pix), device_id_type=MESH)
+    def greet(when, to):
+        @pl.when(when)
+        def _():
+            pl.semaphore_signal(barrier, inc=1, device_id=to, device_id_type=MESH)
+
+    greet(inside & jnp.logical_not(calls_up), (next_chip, pix))
+    greet(inside & jnp.logical_not(calls_up), (two_back, pix))
+    greet(half_later, (two_on, pix))
+    greet(relayed, (inward, pix))
+    greet(relays, (relays_for, 1 - pix))
 
     def loop(count, body):
         lax.fori_loop(0, count, lambda i, carry: (body(i), carry)[1], 0)
 
-    small = [
-        pltpu.make_async_copy(src, dst, small_sem.at[i])
-        for i, (src, dst) in enumerate(
-            ((class_hbm, class_ref), (blur_hbm, blur_ref), (taps_hbm, taps_ref), (mask_hbm, mask_ref))
-        )
-    ]
-    for copy in small:
-        copy.start()
+    small_blur = pltpu.make_async_copy(small_ref.at[pl.ds(rows + 8, 16)], blur_ref, small_sem.at[0])
+    small_blur.start()
+    classes[0] = jnp.broadcast_to(small_ref[rows : rows + 1, :].astype(jnp.int32), (8, WIDTH))
     loop(chunks, lambda c: load_own(c).start())
-    small[0].wait()
-    classes[0] = jnp.broadcast_to(class_ref[...], (8, WIDTH))
-    pl.semaphore_wait(barrier, 2 + inside.astype(jnp.int32) + sends_half.astype(jnp.int32))
-
-    @pl.when(inside)
-    def _():
+    greetings = (inside, sends_half, calls_up, relays, ends)
+    pl.semaphore_wait(barrier, 2 + sum(g.astype(jnp.int32) for g in greetings))
+
+    @pl.when(calls_up)
+    def _():
+        pl.semaphore_signal(ready, inc=1, device_id=(next_chip, pix), device_id_type=MESH)
+        pl.semaphore_signal(ready, inc=1, device_id=(two_back, pix), device_id_type=MESH)
+
+    def first_far():
         class_far.start()
         loop(FAR_AHEAD, lambda c: to_far(c).start())
 
+    @pl.when(inside & jnp.logical_not(far_later))
+    def _():
+        first_far()
+
     class_near.start()
 
-    @pl.when(sends_half)
+    @pl.when(sends_half & jnp.logical_not(half_later))
     def _():
         class_half.start()
 
     low_lanes = lax.broadcasted_iota(jnp.int32, (size // 2, WIDTH), 1) < WIDTH // 2
     rolled_lanes = low_lanes == (core == 0)
 
-    def pack(c):
+    def pack(c, may_send):
         load_own(c).wait()
         to_near(c).start()
         pair = STEP // 2
@@ -136,13 +183,26 @@
         stays = own[pl.ds(base(c) + pair * (1 - core), pair)].reshape(size // 2, WIDTH)
         packed[c] = jnp.where(rolled_lanes, pltpu.roll(moved, WIDTH // 2, 1), stays)
 
-        @pl.when(sends_half)
+        @pl.when(may_send)
         def _():
             to_half(c).start()
 
-    loop(AHEAD, pack)
-    for copy in small[1:]:
-        copy.wait()
+    loop(AHEAD, lambda c: pack(c, sends_half & jnp.logical_not(half_later)))
+
+    @pl.when(follows)
+    def _():
+        pl.semaphore_wait(ready, 1)
+
+    @pl.when(far_later)
+    def _():
+        first_far()
+
+    @pl.when(half_later)
+    def _():
+        class_half.start()
+        loop(AHEAD, lambda c: to_half(c).start())
+
+    small_blur.wait()
 
     blur_high[...] = jnp.zeros_like(blur_high)
     blur_low[...] = jnp.zeros_like(blur_low)
@@ -161,10 +221,12 @@
             blur_high[place] = high
             blur_low[place] = low
 
-    taps = taps_ref.shape[1]
-    for k in range(taps_ref.shape[0]):
+    for k in range(CLASSES):
+        row = rows + 24 + k
         wide = jnp.concatenate(
-            [jnp.broadcast_to(taps_ref[k : k + 1, :], (WIDTH, taps)), jnp.zeros((WIDTH, 5 * WIDTH - taps), F32)], axis=1
+            [jnp.broadcast_to(small_ref[row + 4 * i : row + 4 * i + 1, :], (WIDTH, WIDTH)) for i in range(3)]
+            + [jnp.zeros((WIDTH, 2 * WIDTH), F32)],
+            axis=1,
         )
         wide = pltpu.roll(wide, WIDTH // 2, 1, stride=1, stride_axis=0)
         for block in range(5):
@@ -173,7 +235,7 @@
     def weights(slot, block):
         level = column(classes[slot, 0:1, :])
         total = jnp.zeros((WIDTH, WIDTH), F32)
-        for k in range(taps_ref.shape[0]):
+        for k in range(CLASSES):
             total = total + jnp.where(level == k, stack[k, block], F32(0.0))
         return total
 
@@ -229,7 +291,7 @@
         return banded(c, (far, beyond), 2)
 
     def tissue(c):
-        rows_of = [column(mask_ref[pl.ds(base(c) + r, 1), :].astype(F32)) for r in range(STEP)]
+        rows_of = [column(small_ref[pl.ds(base(c) + r, 1), :]) for r in range(STEP)]
         return jnp.concatenate(rows_of, axis=0)
 
     def window(c, start, groups):
@@ -266,10 +328,11 @@
 
         pass_on(c).start()
 
-    def take_edge():
-        to_edge().wait_recv()
+    def keep_edge():
         keep_spectral(jnp.where(pix == 0, rows + 4, 0), edge_in[...])
-        blur(0)
+
+    def add_out(c, values):
+        out_ref[at(c)] = out_ref[at(c)] + values.reshape(STEP, COLS, WIDTH)
 
     def step(c):
         @pl.when(inside & (c + FAR_AHEAD < chunks))
@@ -278,15 +341,22 @@
 
         @pl.when(c + AHEAD < chunks)
         def _():
-            pack(c + AHEAD)
+            pack(c + AHEAD, sends_half)
 
         @pl.when(c >= 3)
         def _():
             blur(c - 2)
 
-        @pl.when(jnp.logical_not(late) & (c == EDGE_AT))
-        def _():
-            take_edge()
+        @pl.when(relays & (c == RELAY_AT))
+        def _():
+            to_relay().wait_recv()
+            from_relay().start()
+
+        @pl.when(jnp.logical_not(line_end) & (c == EDGE_AT))
+        def _():
+            to_edge().wait_recv()
+            keep_edge()
+            blur(0)
 
         arrive_far(c)
         arrive_near(c)
@@ -299,7 +369,11 @@
         def _():
             edge_out[...] = values
 
-        @pl.when(jnp.logical_not(late) & (c == 0))
+        @pl.when(relayed & (c == 0))
+        def _():
+            to_relay().start()
+
+        @pl.when(jnp.logical_not(line_end) & (c == 0))
         def _():
             to_edge().start()
 
@@ -309,9 +383,18 @@
     blur(last - 2)
     keep_out(last - 1, window(last - 1, 1 - pix, 2))
     keep_out(last, window(last, 2 - 2 * pix, 1))
+
+    @pl.when(line_end)
+    def _():
+        keep_out(0, window(0, pix, 2))
+
     arrive_far(last)
 
-    @pl.when(late)
+    @pl.when(relayed)
+    def _():
+        to_edge_half().start()
+
+    @pl.when(line_end & jnp.logical_not(relayed))
     def _():
         to_edge().start()
 
@@ -321,13 +404,31 @@
     pass_on(last).wait_recv()
     keep_spectral(base(last) + 4, (values + late_part(last)) * cover)
     for c, start in ((last - 1, 2 * pix), (last, 1)):
-        out_ref[at(c)] = out_ref[at(c)] + window(c, start, 1).reshape(STEP, COLS, WIDTH)
-
-    @pl.when(late)
-    def _():
-        take_edge()
-
-    to_edge().wait_send()
+        add_out(c, window(c, start, 1))
+
+    @pl.when(relayed)
+    def _():
+        from_relay().wait_recv()
+        to_edge_half().wait()
+        to_relay().wait_send()
+
+    @pl.when(line_end & jnp.logical_not(relayed))
+    def _():
+        to_edge().wait()
+
+    @pl.when(line_end)
+    def _():
+        keep_edge()
+        add_out(0, window(0, 2 - 2 * pix, 1))
+
+    @pl.when(jnp.logical_not(line_end))
+    def _():
+        to_edge().wait_send()
+
+    @pl.when(relays)
+    def _():
+        from_relay().wait_send()
+
     class_near.wait_send()
     class_on.wait_send()
 
@@ -355,16 +456,27 @@
     slabs = lax.axis_size("mz")
     block = (rows, cols, width)
     dma = pltpu.SemaphoreType.DMA
-    return pl.pallas_call(
-        functools.partial(kernel, slabs, rows),
-        out_shape=jax.ShapeDtypeStruct(block, F32),
-        in_specs=[pl.BlockSpec(memory_space=pltpu.HBM)] * 5,
+    small = pl.pallas_call(
+        gather_small,
+        out_shape=jax.ShapeDtypeStruct((rows + 40, width), F32),
+        in_specs=[pl.BlockSpec(memory_space=pl.ANY)] * 4,
         out_specs=pl.BlockSpec(memory_space=pltpu.VMEM),
         scratch_shapes=[
             pltpu.VMEM(tissue_mask.shape, jnp.int32),
             pltpu.VMEM((1, width), jnp.int32),
+            pltpu.VMEM(blur_taps.shape, F32),
             pltpu.VMEM(peak_taps.shape, F32),
-            pltpu.SMEM(blur_taps.shape, F32),
+            dma((4,)),
+        ],
+        compiler_params=pltpu.CompilerParams(vmem_limit_bytes=60 * 2**20),
+    )(tissue_mask, peak_class.reshape(1, width), blur_taps, peak_taps)
+    return pl.pallas_call(
+        functools.partial(kernel, slabs, rows),
+        out_shape=jax.ShapeDtypeStruct(block, F32),
+        in_specs=[pl.BlockSpec(memory_space=pl.ANY), pl.BlockSpec(memory_space=pltpu.VMEM)],
+        out_specs=pl.BlockSpec(memory_space=pltpu.VMEM),
+        scratch_shapes=[
+            pltpu.SMEM((16, width), F32),
             pltpu.VMEM(block, F32),
             pltpu.VMEM(block, F32),
             pltpu.VMEM(block, F32),
@@ -374,31 +486,33 @@
             pltpu.VMEM(((rows + 8) * cols, 2 * width), BF16),
             pltpu.VMEM((size, (STEP + 8) * cols), BF16),
             pltpu.VMEM((size, (STEP + 8) * cols), BF16),
-            pltpu.VMEM((peak_taps.shape[0], 5, width, width), F32),
+            pltpu.VMEM((CLASSES, 5, width, width), F32),
             pltpu.VMEM((4 * width, 2 * width), BF16),
             pltpu.VMEM((width, 2 * width), BF16),
             pltpu.VMEM((width, 2 * width), BF16),
             pltpu.VMEM((size, width), F32),
             pltpu.VMEM((size, width), F32),
+            pltpu.VMEM((size // 2, width), F32),
             pltpu.VMEM((5, 8, width), jnp.int32),
-            dma((4,)),
-            dma((chunks,)),
-            dma((chunks,)),
-            dma((chunks,)),
-            dma((chunks,)),
-            dma((chunks,)),
-            dma((chunks,)),
-            dma((chunks,)),
-            dma((chunks,)),
-            dma((chunks,)),
             dma((2,)),
+            dma((chunks,)),
+            dma((chunks,)),
+            dma((chunks,)),
+            dma((chunks,)),
+            dma((chunks,)),
+            dma((chunks,)),
+            dma((chunks,)),
+            dma((chunks,)),
+            dma((chunks,)),
+            dma((6,)),
             dma((5,)),
             dma((5,)),
+            pltpu.SemaphoreType.REGULAR,
         ],
         compiler_params=pltpu.CompilerParams(
             collective_id=0, has_side_effects=True, vmem_limit_bytes=48 * 2**20
         ),
-    )(residual, tissue_mask, peak_class.reshape(1, width), peak_taps, blur_taps)
+    )(residual, small)
 
 
 def solution(mesh):

time: 94.2 us -> 90.7 us (0.963)
  local copies, waits for them, and re-layouts: 4.82 us -> 2.82 us
  Pallas kernels: 89.2 us -> 87.7 us
    pallas_call x1, Pallas kernels: 89.2 us -> 86.2 us  [per_device(): pl.pallas_call(functools.partial(kernel, slabs, rows), out_shape=jax.Shap...]
    unnamed x9 -> x3, local copies, waits for them, and re-layouts: 4.82 us -> 2.82 us
    pallas_call x0 -> x1, Pallas kernels: none -> 1.42 us  [per_device(): pl.pallas_call(gather_small, out_shape=jax.ShapeDtypeStruct((rows + 40, w...]
where the time goes in v2:
time: 90.7 us; the launch traced here: 90.5 us
  Pallas kernels  87.7 us (97%)
  local copies, waits for them, and re-layouts  2.82 us (3%)
    pallas_call x1, Pallas kernels, per_device(): pl.pallas_call(functools.partial(kernel, slabs, rows), out_shape=jax.Shap...  86.2 us
    unnamed x3, local copies, waits for them, and re-layouts  2.82 us

profile of v2, /device:TPU:25, one launch (start us, length us, event | category | flops | bytes accessed | tf_op | source)
XLA Modules:
  0.0 90.5 jit_solution(9475067038454527411)
XLA Ops:
  0.0 1.4 %shard_map.55.small_ref = f32[104,128]{1,0:T(8,128)} custom-call(s32[64,128]{1,0:T(8,128)} %mask_hbm.1, s32[1,128]{1,0:T(1,128)} %bitcast.1, f32[9,9]{1,0:T(8,128)} %blur_hbm.1, f32[4,384]{1,0:T(4,128)} %taps_hbm.1), custom_call_target="tpu_custom_call" | custom-call | tf_op jit(solution)/shard_map/pallas_call | solution.py:459
  1.4 0.0 copy-start
  1.4 0.8 copy-done
  2.2 86.2 %shard_map.56 = f32[64,128,128]{2,1,0:T(8,128)S(1)} custom-call(f32[64,128,128]{2,1,0:T(8,128)} %x_ref.1, f32[104,128]{1,0:T(8,128)S(1)} %copy-done), custom_call_target="tpu_custom_call" | custom-call | tf_op jit(solution)/shard_map/pallas_call | solution.py:473
  88.5 2.0 %copy.7 = f32[64,128,128]{2,1,0:T(8,128)} copy(f32[64,128,128]{2,1,0:T(8,128)S(1)} %shard_map.56) | data formatting | bytes 8388608
Async XLA Ops:
  1.4 0.8 copy-start

commit v3 on v2

--- a/solution.py
+++ b/solution.py
@@ -14,9 +14,11 @@
 COLS = 128
 CLASSES = 4
 STEP = 4
+ROOM = 32768
 AHEAD = 3
-FAR_AHEAD = 4
-RELAY_AT = 7
+FAR_AHEAD = 8
+RELAYED = 2
+RELAY_AT = 10
 EDGE_AT = 14
 LINE = 16
 
@@ -34,7 +36,7 @@
     return jnp.broadcast_to(row, (WIDTH, row.shape[1])).T
 
 
-def gather_small(mask_hbm, class_hbm, blur_hbm, taps_hbm, out_ref, mask_ref, class_ref, blur_ref, taps_ref, sems):
+def gather_small(mask_hbm, class_hbm, blur_hbm, taps_hbm, out_hbm, out_ref, mask_ref, class_ref, blur_ref, taps_ref, sems):
     pairs = ((mask_hbm, mask_ref), (class_hbm, class_ref), (blur_hbm, blur_ref), (taps_hbm, taps_ref))
     copies = [pltpu.make_async_copy(src, dst, sems.at[i]) for i, (src, dst) in enumerate(pairs)]
     for copy in copies:
@@ -47,11 +49,14 @@
     out_ref[rows + 8 : rows + 17, :9] = blur_ref[...]
     for i in range(3):
         out_ref[rows + 24 + 4 * i : rows + 28 + 4 * i] = taps_ref[:, i * WIDTH : (i + 1) * WIDTH]
+    back = pltpu.make_async_copy(out_ref, out_hbm.at[pl.ds(0, out_ref.shape[0])], sems.at[4])
+    back.start()
+    back.wait()
 
 
 def kernel(
     slabs, rows,
-    x_ref, small_ref, out_ref, blur_ref, own, far, near, beyond, half, packed, spectral, blur_high, blur_low,
+    x_ref, small_hbm, out_ref, small_ref, blur_ref, own, far, near, beyond, half, packed, spectral, blur_high, blur_low,
     stack, band, half_high, half_low, edge_out, edge_in, relay, classes,
     small_sem, own_sem, far_send, far_recv, near_send, near_recv, on_send, on_recv,
     half_send, half_recv, edge_sems, class_send, class_recv, ready,
@@ -109,9 +114,9 @@
     def to_edge():
         return remote(edge_out, edge_in, edge_sems.at[0], edge_sems.at[1], (m, 1 - pix))
 
-    first, second = pl.ds(0, size // 2), pl.ds(size // 2, size // 2)
-
-    def to_edge_half():
+    first, second = pl.ds(0, RELAYED * COLS), pl.ds(RELAYED * COLS, size - RELAYED * COLS)
+
+    def to_edge_rest():
         return remote(edge_out.at[second], edge_in.at[second], edge_sems.at[0], edge_sems.at[1], (m, 1 - pix))
 
     def to_relay():
@@ -146,10 +151,11 @@
     def loop(count, body):
         lax.fori_loop(0, count, lambda i, carry: (body(i), carry)[1], 0)
 
-    small_blur = pltpu.make_async_copy(small_ref.at[pl.ds(rows + 8, 16)], blur_ref, small_sem.at[0])
+    small = pltpu.make_async_copy(small_hbm.at[pl.ds(0, rows + 40)], small_ref, small_sem.at[0])
+    small_blur = pltpu.make_async_copy(small_hbm.at[pl.ds(rows + 8, 16)], blur_ref, small_sem.at[1])
+    small.start()
     small_blur.start()
-    classes[0] = jnp.broadcast_to(small_ref[rows : rows + 1, :].astype(jnp.int32), (8, WIDTH))
-    loop(chunks, lambda c: load_own(c).start())
+
     greetings = (inside, sends_half, calls_up, relays, ends)
     pl.semaphore_wait(barrier, 2 + sum(g.astype(jnp.int32) for g in greetings))
 
@@ -158,15 +164,23 @@
         pl.semaphore_signal(ready, inc=1, device_id=(next_chip, pix), device_id_type=MESH)
         pl.semaphore_signal(ready, inc=1, device_id=(two_back, pix), device_id_type=MESH)
 
-    def first_far():
+    @pl.when(inside & jnp.logical_not(far_later))
+    def _():
+        to_far(0).start()
+
+    small.wait()
+    classes[0] = jnp.broadcast_to(small_ref[rows : rows + 1, :].astype(jnp.int32), (8, WIDTH))
+
+    def rest_of_far():
         class_far.start()
-        loop(FAR_AHEAD, lambda c: to_far(c).start())
+        lax.fori_loop(1, FAR_AHEAD, lambda c, carry: (to_far(c).start(), carry)[1], 0)
 
     @pl.when(inside & jnp.logical_not(far_later))
     def _():
-        first_far()
+        rest_of_far()
 
     class_near.start()
+    loop(chunks, lambda c: load_own(c).start())
 
     @pl.when(sends_half & jnp.logical_not(half_later))
     def _():
@@ -195,7 +209,8 @@
 
     @pl.when(far_later)
     def _():
-        first_far()
+        to_far(0).start()
+        rest_of_far()
 
     @pl.when(half_later)
     def _():
@@ -392,7 +407,7 @@
 
     @pl.when(relayed)
     def _():
-        to_edge_half().start()
+        to_edge_rest().start()
 
     @pl.when(line_end & jnp.logical_not(relayed))
     def _():
@@ -409,7 +424,7 @@
     @pl.when(relayed)
     def _():
         from_relay().wait_recv()
-        to_edge_half().wait()
+        to_edge_rest().wait()
         to_relay().wait_send()
 
     @pl.when(line_end & jnp.logical_not(relayed))
@@ -458,24 +473,26 @@
     dma = pltpu.SemaphoreType.DMA
     small = pl.pallas_call(
         gather_small,
-        out_shape=jax.ShapeDtypeStruct((rows + 40, width), F32),
+        out_shape=jax.ShapeDtypeStruct((ROOM, width), F32),
         in_specs=[pl.BlockSpec(memory_space=pl.ANY)] * 4,
-        out_specs=pl.BlockSpec(memory_space=pltpu.VMEM),
+        out_specs=pl.BlockSpec(memory_space=pl.ANY),
         scratch_shapes=[
+            pltpu.VMEM((rows + 40, width), F32),
             pltpu.VMEM(tissue_mask.shape, jnp.int32),
             pltpu.VMEM((1, width), jnp.int32),
             pltpu.VMEM(blur_taps.shape, F32),
             pltpu.VMEM(peak_taps.shape, F32),
-            dma((4,)),
+            dma((5,)),
         ],
         compiler_params=pltpu.CompilerParams(vmem_limit_bytes=60 * 2**20),
     )(tissue_mask, peak_class.reshape(1, width), blur_taps, peak_taps)
     return pl.pallas_call(
         functools.partial(kernel, slabs, rows),
         out_shape=jax.ShapeDtypeStruct(block, F32),
-        in_specs=[pl.BlockSpec(memory_space=pl.ANY), pl.BlockSpec(memory_space=pltpu.VMEM)],
+        in_specs=[pl.BlockSpec(memory_space=pl.ANY)] * 2,
         out_specs=pl.BlockSpec(memory_space=pltpu.VMEM),
         scratch_shapes=[
+            pltpu.VMEM((rows + 40, width), F32),
             pltpu.SMEM((16, width), F32),
             pltpu.VMEM(block, F32),
             pltpu.VMEM(block, F32),
@@ -492,7 +509,7 @@
             pltpu.VMEM((width, 2 * width), BF16),
             pltpu.VMEM((size, width), F32),
             pltpu.VMEM((size, width), F32),
-            pltpu.VMEM((size // 2, width), F32),
+            pltpu.VMEM((RELAYED * cols, width), F32),
             pltpu.VMEM((5, 8, width), jnp.int32),
             dma((2,)),
             dma((chunks,)),

time: 90.7 us -> 90.4 us (level)
    unnamed x3 -> x1, local copies, waits for them, and re-layouts: 2.82 us -> 2.02 us
where the time goes in v3:
time: 90.4 us; the launch traced here: 90.2 us
  Pallas kernels  88.2 us (98%)
  local copies, waits for them, and re-layouts  2.02 us (2%)
    pallas_call x1, Pallas kernels, per_device(): pl.pallas_call(functools.partial(kernel, slabs, rows), out_shape=jax.Shap...  86.8 us
    unnamed x1, local copies, waits for them, and re-layouts  2.02 us

profile of v3, /device:TPU:25, one launch (start us, length us, event | category | flops | bytes accessed | tf_op | source)
XLA Modules:
  0.0 90.2 jit_solution(1547804994069077047)
XLA Ops:
  0.0 1.4 %shard_map.55.small_hbm = f32[32768,128]{1,0:T(8,128)} custom-call(s32[64,128]{1,0:T(8,128)} %mask_hbm.1, s32[1,128]{1,0:T(1,128)} %bitcast.1, f32[9,9]{1,0:T(8,128)} %blur_hbm.1, f32[4,384]{1,0:T(4,128)} %taps_hbm.1), custom_call_target="tpu_custom_call" | custom-call | tf_op jit(solution)/shard_map/pallas_call | solution.py:474
  1.4 86.8 %shard_map.56 = f32[64,128,128]{2,1,0:T(8,128)S(1)} custom-call(f32[64,128,128]{2,1,0:T(8,128)} %x_ref.1, f32[32768,128]{1,0:T(8,128)} %shard_map.55.small_hbm), custom_call_target="tpu_custom_call" | custom-call | tf_op jit(solution)/shard_map/pallas_call | solution.py:489
  88.2 2.0 %copy.7 = f32[64,128,128]{2,1,0:T(8,128)} copy(f32[64,128,128]{2,1,0:T(8,128)S(1)} %shard_map.56) | data formatting | bytes 8388608
